TPU v7x, 32 devices: a whole 2x2x4 slice. The times are simulated.
32 devices in a mesh: dom: 4 (over x, core), shard: 8 (over z, y).
Axes of the slice: x: 2, y: 2, z: 4, core: 2. Of those that a mesh axis runs over, the one named last changes fastest.
Arguments:
- embeddings: float32 [2048, 400], P(('dom', 'shard')), may hold values from -3 to 3
- row_accum: float32 [2048], P(('dom', 'shard')), may hold values from 0.01 to 1
- relations: bfloat16 [160, 400], replicated, may hold values from -3 to 3
- relation_accum: float32 [160], P(('dom', 'shard')), may hold values from 0.01 to 1
- request_rows: int32 [2, 256, 2, 16], P(None, ('dom', 'shard')), may hold values from 0 to 63
- head_slots: int32 [2, 4096], P(None, ('dom', 'shard')), may hold values from 0 to 127
- tail_slots: int32 [2, 4096], P(None, ('dom', 'shard')), may hold values from 0 to 127
- relation_ids: int32 [2, 4096], P(None, ('dom', 'shard')), may hold values from 0 to 159
- own_negatives: int32 [2, 16384], P(None, ('dom', 'shard')), may hold values from 0 to 127
- far_negatives: int32 [2, 16384], P(None, ('dom', 'shard')), may hold values from 0 to 127
Outputs:
- new_embeddings: float32 [2048, 400], P(('dom', 'shard'))
- new_accum: float32 [2048], P(('dom', 'shard'))
- relation_step: float32 [160, 400], P(('dom', 'shard'))
- new_relation_accum: float32 [160], P(('dom', 'shard'))
Inputs may be any that keep to these rules, and one draw needn't show every extreme that they name: `request_rows`: local row numbers within the owner's 64 rows. `head_slots`: slots of the 128 own-side touched rows. `tail_slots`: slots of the 128 partner-side touched rows. `own_negatives`: slots of the 128 own-side touched rows. `far_negatives`: slots of the 128 partner-side touched rows.
All inputs are finite; a program needn't handle non-finite values.
Results may differ from a plain program's by a relative error of at most 0.0049.
Values may be sent and summed in bfloat16 or wider, within the bound.
No kernel may reach another device: no remote copies, remote signals or barrier semaphores. Data moves between devices by JAX's collectives and lax.ppermute only.
A program may use at most 64 MiB of HBM per device.

v0:
```python
import functools

import jax
import jax.numpy as jnp
from jax import lax
from jax.experimental import pallas as pl
from jax.experimental.pallas import tpu as pltpu
from jax.sharding import PartitionSpec as P

LEARN_RATE = 0.1
LANES = 128
VMEM_LIMIT = 48 * 2**20
BF16 = jnp.bfloat16
F32 = jnp.float32
NATURAL = (((1,), (0,)), ((), ()))
LAST = (((1,), (1,)), ((), ()))
FIRST = (((0,), (0,)), ((), ()))
HBM = pl.BlockSpec(memory_space=pltpu.HBM)
VMEM = pl.BlockSpec(memory_space=pltpu.VMEM)


def dot(left, right, dims=NATURAL):
    return lax.dot_general(left, right, dims, preferred_element_type=F32)


def iota(shape, axis):
    return lax.broadcasted_iota(jnp.int32, shape, axis)


def one_hot_t(row, count):
    return (iota((count, row.shape[1]), 0) == row).astype(BF16)


def one_hot(column, count):
    return (iota((column.shape[0], count), 1) == column.astype(jnp.int32)).astype(BF16)


def to_column(row):
    n = row.shape[1]
    same = iota((n, n), 0) == iota((n, n), 1)
    return jnp.sum(jnp.where(same, row.astype(F32), 0.0), axis=1, keepdims=True)


def to_row(column):
    n = column.shape[0]
    return jnp.sum(jnp.where(iota((n, n), 0) == iota((n, n), 1), column, 0.0), axis=0, keepdims=True)


def reverse(index, count):
    return (count - 1) ^ index


def spread_order(shards):
    return [reverse(s, shards) for s in range(shards)]


def group_bit(r):
    return 1 - ((lax.axis_index("dom") >> r) & 1)


def renumber(slot, shards, slots):
    half = slots // 2
    return (slot // half % 2) * (shards * half) + reverse(slot // slots, shards) * half + slot % half


def halves(ref, r):
    rows, bit = ref.shape[0] // 2, group_bit(r)
    return [pl.ds(pl.multiple_of(side * rows, rows), rows) for side in (bit, 1 - bit)]


def whole(width):
    return width // LANES * LANES


def unfold(value, width):
    tiles, rest = whole(width), width - whole(width)
    return jnp.concatenate(
        [
            jnp.concatenate(
                [value[:, side * tiles : (side + 1) * tiles], value[:, 2 * tiles + side * rest :][:, :rest]], axis=1
            )
            for side in range(2)
        ],
        axis=0,
    )


def beside(left, right):
    tiles = whole(left.shape[1])
    return jnp.concatenate([left[:, :tiles], right[:, :tiles], left[:, tiles:], right[:, tiles:]], axis=1)


def fold(value):
    n = value.shape[0] // 2
    return beside(value[:n], value[n:])


def request_columns(request_ref, r):
    _, shards, _, slots = request_ref.shape
    half = slots // 2
    sides = [request_ref[r, :, k, :].astype(F32) for k in range(2)]
    flip = group_bit(r) == 1
    rep = jnp.concatenate(
        [
            jnp.broadcast_to(ids[reverse(place, shards)][None], (half, slots))
            for ids in (jnp.where(flip, sides[1], sides[0]), jnp.where(flip, sides[0], sides[1]))
            for place in range(shards)
        ],
        axis=0,
    )
    n = rep.shape[0]
    lane, inside = iota((n, slots), 1), iota((n, slots), 0) % half
    return [
        jnp.sum(jnp.where(lane == side * half + inside, rep, 0.0), axis=1, keepdims=True) for side in range(2)
    ]


def serve(request_ref, r, table, out_ref):
    rows, width = table.shape
    table = table.astype(BF16)
    hot = jnp.concatenate([one_hot(column, rows) for column in request_columns(request_ref, r)], axis=1)
    blank = jnp.zeros((rows, width), BF16)
    both = jnp.concatenate([beside(table, blank), beside(blank, table)], axis=0)
    out_ref[...] = dot(hot, both).astype(BF16)


def first_kernel(request_ref, state_ref, *refs):
    out_ref = refs[-1]
    table = state_ref[: state_ref.shape[0] - 2]
    serve(request_ref, 0, table, out_ref)


def request_hot(request_ref, r, rows):
    return jnp.concatenate([one_hot(column, rows) for column in request_columns(request_ref, r)], axis=0)


def row_update(hot, back_ref, state_ref, dims=FIRST):
    rows, width = state_ref.shape[0] - 2, state_ref.shape[1]
    row_grad = dot(hot, unfold(back_ref[:, : 2 * width], width), dims)
    accum = to_column(state_ref[rows : rows + 1, :rows]) + jnp.mean(row_grad * row_grad, axis=1, keepdims=True)
    return state_ref[:rows] - row_grad * (LEARN_RATE * lax.rsqrt(accum)), to_row(accum)


def middle_kernel(r, request_ref, back_ref, state_ref, state_out, out_ref):
    rows = state_ref.shape[0] - 2
    table, accum = row_update(request_hot(request_ref, r, rows), back_ref, state_ref)
    serve(request_ref, r + 1, table, out_ref)
    state_out[:rows] = table
    state_out[rows:] = state_ref[rows:]
    state_out[rows : rows + 1, :rows] = accum


def slots_of(ref):
    return 2 * ref.shape[0] // (2 * lax.axis_size("shard"))


def by_blocks(function, *arrays):
    step = 16
    parts = [function(*[x[i : i + step] for x in arrays]) for i in range(0, arrays[0].shape[0], step)]
    return [jnp.concatenate(column, axis=0) for column in zip(*parts)]


def query_block(head, tail, rel):
    tail_query = head * rel
    positive = jnp.sum(tail_query * tail, axis=1, keepdims=True)
    return tail_query.astype(BF16), (tail * rel).astype(BF16), -jax.nn.sigmoid(-positive)


def grad_block(head, tail, rel, coeff, back_tail, back_head):
    toward_head = coeff * tail + back_tail
    grad_rel = head * toward_head + tail * back_head
    return (
        (rel * toward_head).astype(BF16),
        (rel * (coeff * head + back_head)).astype(BF16),
        grad_rel.astype(BF16),
    )


def edge_kernel(
    r,
    bit,
    per_device,
    rec_ref,
    head_ref,
    tail_ref,
    rel_ref,
    own_neg_ref,
    far_neg_ref,
    relations_ref,
    *refs,
):
    width = relations_ref.shape[1]
    shards, slots = lax.axis_size("shard"), slots_of(rec_ref)
    touched = shards * slots
    edges, negatives = head_ref.shape[1], own_neg_ref.shape[1]
    own_half, far_half = halves(rec_ref, r)
    own = unfold(rec_ref[own_half], width)
    far = unfold(rec_ref[far_half], width)
    row = slice(r, r + 1)
    ids = rel_ref[row]
    heads, tails = renumber(head_ref[row], shards, slots), renumber(tail_ref[row], shards, slots)
    head = dot(one_hot(to_column(heads), touched), own)
    tail = dot(one_hot(to_column(tails), touched), far)
    rel = dot(one_hot(to_column(ids), relations_ref.shape[0]), relations_ref[...])
    query_tail, query_head, coeff = by_blocks(query_block, head, tail, rel)

    def weights(query, rows, neg_ref):
        hit = iota((touched, negatives), 0) == renumber(neg_ref[row], shards, slots)
        scale = jnp.sum(jnp.where(hit, 1.0 / negatives, 0.0), axis=1, keepdims=True)
        return jax.nn.sigmoid(dot(query, rows, LAST)) * to_row(scale)

    weight_tail = weights(query_tail, far, far_neg_ref)
    weight_head = weights(query_head, own, own_neg_ref)
    back_tail = dot(weight_tail.astype(BF16), far)
    back_head = dot(weight_head.astype(BF16), own)
    grad_head, grad_tail, grad_rel = by_blocks(grad_block, head, tail, rel, coeff, back_tail, back_head)
    right = [
        jnp.concatenate([grad_head, query_head], axis=0),
        jnp.concatenate([grad_tail, query_tail], axis=0),
    ]
    if r < bit:
        out_ref, grad_rel_out = refs
        sides = (own_half, heads, weight_head), (far_half, tails, weight_tail)
        for (half, slot, weight), grads in zip(sides, right):
            out_ref[half] = row_grads(slot, weight, grads)
        grad_rel_out[...] = grad_rel
    else:
        *before_refs, weights_out, right_out, values_out, sums_out = refs
        for side, weight in enumerate((weight_head, weight_tail)):
            weights_out[side], right_out[side] = weight.astype(BF16), right[side]
        values = jnp.concatenate([ref[...] for ref in before_refs] + [grad_rel], axis=0)
        values_out[...] = values
        masks = other_doms(bit)
        for i, mask in enumerate(masks):
            sums_out[i] = relation_sums(rel_ref, values, bit, per_device, mask, rec_ref.shape[0]).astype(BF16)


def other_doms(bit):
    return [mask for mask in range(1, lax.axis_size("dom")) if not mask >> bit & 1]


def relation_sums(rel_ref, values, bit, per_device, mask, rows):
    shards = lax.axis_size("shard")
    ids = jnp.concatenate([rel_ref[r : r + 1] for r in range(rel_ref.shape[0])], axis=1)
    owner = ids // per_device
    dom = owner // shards
    chunk = (1 - (dom >> bit & 1)) * shards + reverse(owner % shards, shards)
    meant = (dom ^ lax.axis_index("dom") ^ mask) & ~(1 << bit) == 0
    rows_each = rows // (2 * shards)
    spot, free = ids % per_device, rows_each - per_device
    hot = one_hot_t(
        jnp.concatenate(
            [
                jnp.where(meant, chunk * rows_each + spot, -1),
                jnp.where(meant, chunk * rows_each + per_device + spot % free, -1),
            ],
            axis=1,
        ),
        rows,
    )
    third = values[:, 2 * LANES : 3 * LANES].astype(F32)
    first = to_column(spot) < free
    split = [jnp.where(first, third, 0.0).astype(BF16), jnp.where(first, 0.0, third).astype(BF16)]
    right = jnp.concatenate([values[:, : 2 * LANES], jnp.concatenate(split, axis=1)], axis=0)
    rest = dot(hot[:, : values.shape[0]], values[:, 3 * LANES :])
    return jnp.concatenate([dot(hot, right), rest], axis=1)


def unpack_sums(total, per_device):
    free = total.shape[0] - per_device
    third = jnp.concatenate(
        [total[per_device:, :LANES], total[per_device : 2 * per_device - free, LANES : 2 * LANES]], axis=0
    )
    return jnp.concatenate([total[:per_device, : 2 * LANES], third, total[:per_device, 2 * LANES :]], axis=1)


def row_grads(slot, weight, grads):
    left = jnp.concatenate([one_hot_t(slot, weight.shape[1]), weight.T.astype(BF16)], axis=1)
    return fold(dot(left, grads).astype(BF16))


def grad_kernel(
    bit,
    per_device,
    request_ref,
    head_ref,
    tail_ref,
    rel_ref,
    weights_ref,
    right_ref,
    values_ref,
    out_ref,
    sums_out,
    hot_out,
):
    shards, slots = lax.axis_size("shard"), slots_of(out_ref)
    for side, (half, slot_ref) in enumerate(zip(halves(out_ref, bit), (head_ref, tail_ref))):
        slot = renumber(slot_ref[bit : bit + 1], shards, slots)
        out_ref[half] = row_grads(slot, weights_ref[side].astype(F32), right_ref[side])
    sums_out[...] = relation_sums(rel_ref, values_ref[...], bit, per_device, 0, out_ref.shape[0])
    hot_out[...] = request_hot(request_ref, bit, hot_out.shape[0]).astype(F32).T.astype(BF16)


def sums_width(width):
    return width - LANES


def wide(width):
    return 2 * whole(width) + 3 * LANES


def join_kernel(grads_ref, sums_ref, *refs):
    *came_refs, out_ref = refs
    tiles = out_ref.shape[1] - 3 * LANES
    total = sums_ref[...]
    for ref in came_refs:
        total = total + ref[...].astype(F32)
    total = total.astype(BF16)
    rests = jnp.concatenate([grads_ref[:, tiles:], total[:, 2 * LANES :]], axis=1)
    blank = jnp.zeros((total.shape[0], LANES - rests.shape[1]), BF16)
    out_ref[:, :tiles] = grads_ref[:, :tiles]
    out_ref[:, tiles : tiles + LANES] = jnp.concatenate([rests, blank], axis=1)
    out_ref[:, tiles + LANES :] = total[:, : 2 * LANES]


def last_kernel(hot_ref, back_ref, state_ref, table_out, row_accum_out, step_out, accum_out, *scratch):
    table_ref, row_accum_ref, step_ref, new_accum_ref, sems = scratch
    pairs = (
        (table_ref, table_out),
        (row_accum_ref, row_accum_out),
        (step_ref, step_out),
        (new_accum_ref, accum_out),
    )
    copies = [pltpu.make_async_copy(source, target, sems.at[i]) for i, (source, target) in enumerate(pairs)]
    table, accum = row_update(hot_ref[...], back_ref, state_ref, NATURAL)
    table_ref[...] = table
    copies[0].start()
    row_accum_ref[...] = accum
    copies[1].start()
    per_device, width = step_ref.shape
    rows = slots_of(back_ref) // 2
    tiles, rest = 2 * whole(width), width - whole(width)
    parts = jnp.concatenate(
        [back_ref[:, tiles + LANES :], back_ref[:, tiles + 2 * rest : tiles + 3 * rest]], axis=1
    ).astype(F32)
    total = jnp.sum(parts.reshape(parts.shape[0] // rows, rows, parts.shape[1]), axis=0)
    grad = unpack_sums(total, per_device)
    accum = to_column(state_ref[table.shape[0] + 1 :, :per_device]) + jnp.mean(grad * grad, axis=1, keepdims=True)
    step_ref[...] = grad * (-LEARN_RATE * lax.rsqrt(accum))
    copies[2].start()
    new_accum_ref[...] = to_row(accum)
    copies[3].start()
    for copy in copies:
        copy.wait()


def call(kernel, outs, *args, **kwargs):
    return pl.pallas_call(
        kernel,
        out_shape=[jax.ShapeDtypeStruct(shape, kind) for shape, kind in outs],
        compiler_params=pltpu.CompilerParams(vmem_limit_bytes=VMEM_LIMIT),
        **kwargs,
    )(*args)


def swap_pair(value, r):
    doms, shards = lax.axis_size("dom"), lax.axis_size("shard")
    order = spread_order(shards)
    groups = [
        [g * shards + s for g in (low ^ (1 << r), low) for s in sorted(range(shards), key=order.__getitem__)]
        for low in range(doms)
        if not low >> r & 1
    ]
    return lax.all_to_all(
        value, ("dom", "shard"), split_axis=0, concat_axis=0, axis_index_groups=groups, tiled=True
    )


def body(
    embeddings,
    row_accum,
    relations,
    relation_accum,
    request_rows,
    head_slots,
    tail_slots,
    relation_ids,
    own_negatives,
    far_negatives,
):
    rows, width = embeddings.shape
    doms, shards = lax.axis_size("dom"), lax.axis_size("shard")
    rounds, slots = request_rows.shape[0], request_rows.shape[-1]
    bit = rounds - 1
    per_device = relation_accum.shape[0]
    assert 3 * (width % LANES) <= LANES
    count, touched = head_slots.shape[1], shards * slots
    free = slots // 2 - per_device
    assert free < per_device <= 2 * free and whole(width) == 3 * LANES
    chunks = ((touched, 2 * width), BF16)
    state = (
        jnp.pad(embeddings, ((0, 2), (0, 0)))
        + jnp.pad(row_accum[None], ((rows, 1), (0, width - rows)))
        + jnp.pad(relation_accum[None], ((rows + 1, 0), (0, width - per_device)))
    )
    edges = (head_slots, tail_slots, relation_ids, own_negatives, far_negatives, relations)
    (outgoing,) = call(first_kernel, [chunks], request_rows, state, *edges)
    before = []
    for r in range(bit):
        received = swap_pair(outgoing, r)
        grads, grad_rel = call(
            functools.partial(edge_kernel, r, bit, per_device), [chunks, ((count, width), BF16)], received, *edges
        )
        before.append(grad_rel)
        back = swap_pair(grads, r)
        state, outgoing = call(
            functools.partial(middle_kernel, r), [(state.shape, F32), chunks], request_rows, back, state
        )
    received = swap_pair(outgoing, bit)
    masks = other_doms(bit)
    weights, right, values, sums = call(
        functools.partial(edge_kernel, bit, bit, per_device),
        [
            ((2, count, touched), BF16),
            ((2, 2 * count, width), BF16),
            ((rounds * count, width), BF16),
            ((len(masks), touched, sums_width(width)), BF16),
        ],
        received,
        *edges,
        *before,
    )
    came = [lax.ppermute(sums[i], "dom", [(g, g ^ mask) for g in range(doms)]) for i, mask in enumerate(masks)]
    grads, sums, hot = call(
        functools.partial(grad_kernel, bit, per_device),
        [chunks, ((touched, sums_width(width)), F32), ((rows, 2 * touched), BF16)],
        request_rows,
        head_slots,
        tail_slots,
        relation_ids,
        weights,
        right,
        values,
    )
    (grads,) = call(join_kernel, [((touched, wide(width)), BF16)], grads, sums, *came)
    back = swap_pair(grads, bit)
    outs = [((rows, width), F32), ((1, rows), F32), ((per_device, width), F32), ((1, per_device), F32)]
    table, accum, step, relation_accum = call(
        last_kernel,
        outs,
        hot,
        back,
        state,
        in_specs=[VMEM] * 3,
        out_specs=[HBM] * 4,
        scratch_shapes=[pltpu.VMEM(*out) for out in outs] + [pltpu.SemaphoreType.DMA((4,))],
    )
    return (table, accum.reshape(rows), step, relation_accum.reshape(per_device))


def solution(mesh):
    placed = (
        P(("dom", "shard"), None),
        P(("dom", "shard")),
        P(),
        P(("dom", "shard")),
        P(None, ("dom", "shard"), None, None),
        P(None, ("dom", "shard")),
        P(None, ("dom", "shard")),
        P(None, ("dom", "shard")),
        P(None, ("dom", "shard")),
        P(None, ("dom", "shard")),
    )
    return jax.shard_map(
        body,
        mesh=mesh,
        in_specs=placed,
        out_specs=(
            P(("dom", "shard"), None),
            P(("dom", "shard")),
            P(("dom", "shard"), None),
            P(("dom", "shard")),
        ),
        check_vma=False,
    )
```

profile of v0, /device:TPU:0, one launch (start us, length us, event | category | flops | bytes accessed | tf_op | source)
XLA Modules:
  0.0 59.4 jit_solution(6162707317843131692)
XLA Ops:
  0.6 0.0 copy-start
  0.6 0.0 copy-start.1
  0.7 0.0 copy-start.2
  0.7 0.0 copy-start.3
  0.7 0.0 copy-start.4
  0.7 0.0 copy-start.5
  0.7 0.0 copy-start.6
  0.7 1.0 %pad_add_fusion.state_ref = f32[66,400]{1,0:T(8,128)S(1)} fusion(f32[1,5]{1,0:T(1,128)} %bitcast.22, f32[1,64]{1,0:T(1,128)} %bitcast.23, f32[64,400]{1,0:T(8,128)} %param.10), kind=kLoop, calls=%fused_computation | loop fusion | flops 52800 | bytes 208276 | tf_op jit(solution)/shard_map/add | solution.py:402
  1.7 0.0 copy-done
  1.8 0.0 copy-done.1
  1.8 0.0 copy-done.2
  1.8 0.0 copy-done.3
  1.8 0.0 copy-done.4
  1.8 0.0 copy-done.5
  1.8 0.0 copy-done.6
  1.8 0.4 shard_map.129
  2.2 13.8 %all_to_all.44 = bf16[16,8,800]{2,1,0:T(8,128)(2,1)S(1)} all-to-all(bf16[16,8,800]{2,1,0:T(8,128)(2,1)S(1)} %bitcast.16), channel_id=1, replica_groups={{15,14,13,12,11,10,9,8,7,6,5,4,3,2,1,0},{31,30,29,28,27,26,25,24,23,22,..., dimensions={0} | all-to-all | bytes 409600 | tf_op jit(solution)/shard_map/all_to_all | solution.py:374
  16.0 1.0 %shard_map.130 = (bf16[128,800]{1,0:T(8,128)(2,1)S(1)}, bf16[128,400]{1,0:T(8,128)(2,1)S(1)}) custom-call(bf16[128,800]{1,0:T(8,128)(2,1)S(1)} %bitcast.15, s32[2,128]{1,0:T(2,128)S(1)} %copy-done.4, s32[2,128]{1,0:T(2,128)S(1)} %copy-done.5, s32[2,128]{1,0:T(2,128)S(1)} %copy-done.6, s32[2,512]{1,0:T(2,128)S(1)} %copy-done.2, s32[2,512]{1,0:T(2,128)S(1)} %copy-done.3, ...), custom_call_target="tpu_custom_call" | custom-call | tf_op jit(solution)/shard_map/pallas_call | solution.py:358
  17.1 11.6 %all_to_all.45 = bf16[16,8,800]{2,1,0:T(8,128)(2,1)S(1)} all-to-all(bf16[16,8,800]{2,1,0:T(8,128)(2,1)S(1)} %bitcast.20), channel_id=1, replica_groups={{15,14,13,12,11,10,9,8,7,6,5,4,3,2,1,0},{31,30,29,28,27,26,25,24,23,22,..., dimensions={0} | all-to-all | bytes 409600 | tf_op jit(solution)/shard_map/all_to_all | solution.py:374
  28.6 0.6 shard_map.131
  29.2 12.8 %all_to_all.46 = bf16[16,8,800]{2,1,0:T(8,128)(2,1)S(1)} all-to-all(bf16[16,8,800]{2,1,0:T(8,128)(2,1)S(1)} %bitcast.19), channel_id=1, replica_groups={{23,22,21,20,19,18,17,16,7,6,5,4,3,2,1,0},{31,30,29,28,27,26,25,24,15,1..., dimensions={0} | all-to-all | bytes 409600 | tf_op jit(solution)/shard_map/all_to_all | solution.py:374
  42.0 1.0 %shard_map.132 = (bf16[2,128,128]{2,1,0:T(8,128)(2,1)S(1)}, bf16[2,256,400]{2,1,0:T(8,128)(2,1)S(1)}, bf16[256,400]{1,0:T(8,128)(2,1)S(1)}, bf16[1,128,272]{2,1,0:T(8,128)(2,1)S(1)}) custom-call(bf16[128,800]{1,0:T(8,128)(2,1)S(1)} %bitcast.17, s32[2,128]{1,0:T(2,128)S(1)} %copy-done.4, s32[2,128]{1,0:T(2,128)S(1)} %copy-done.5, s32[2,128]{1,0:T(2,128)S(1)} %copy-done.6, ...), custom_call_target="tpu_custom_call" | custom-call | tf_op jit(solution)/shard_map/pallas_call | solution.py:358
  43.0 0.1 collective-permute-start
  43.1 0.4 shard_map.133
  43.5 0.9 %collective-permute-done.refs_0_ = bf16[128,272]{1,0:T(8,128)(2,1)S(1)} collective-permute-done((bf16[128,272]{1,0:T(8,128)(2,1)S(1)}, bf16[128,272]{1,0:T(8,128)(2,1)S(1)}, u32[]{:S(2)}, u32[]{:S(2)}) %collective-permute-start) | collective-permute-done | bytes 69664 | tf_op jit(solution)/shard_map/ppermute | solution.py:433
  44.4 0.1 shard_map.134
  44.5 14.0 %all_to_all.47 = bf16[16,8,1152]{2,1,0:T(8,128)(2,1)S(1)} all-to-all(bf16[16,8,1152]{2,1,0:T(8,128)(2,1)S(1)} %bitcast.13), channel_id=1, replica_groups={{23,22,21,20,19,18,17,16,7,6,5,4,3,2,1,0},{31,30,29,28,27,26,25,24,15,1..., dimensions={0} | all-to-all | bytes 589824 | tf_op jit(solution)/shard_map/all_to_all | solution.py:374
  58.4 1.0 %shard_map.135 = (f32[64,400]{1,0:T(8,128)}, f32[1,64]{1,0:T(1,128)}, f32[5,400]{1,0:T(8,128)}, f32[1,5]{1,0:T(1,128)}) custom-call(bf16[64,256]{1,0:T(8,128)(2,1)S(1)} %get-tuple-element.25.hot_ref, bf16[128,1152]{1,0:T(8,128)(2,1)S(1)} %bitcast.14, f32[66,400]{1,0:T(8,128)S(1)} %get-tuple-element.29.state_ref), custom_call_target="tpu_custom_call" | custom-call | tf_op jit(solution)/shard_map/pallas_call | solution.py:358
Async XLA Ops:
  0.6 1.1 %copy-start = (bf16[160,400]{1,0:T(8,128)(2,1)S(1)}, bf16[160,400]{1,0:T(8,128)(2,1)}, u32[]{:S(2)}) copy-start(bf16[160,400]{1,0:T(8,128)(2,1)} %relations_ref.3) | copy-start | bytes 384004
  0.6 1.1 %copy-start.1 = (s32[2,8,2,16]{3,2,1,0:T(2,128)S(1)}, s32[2,8,2,16]{3,2,1,0:T(2,128)}, u32[]{:S(2)}) copy-start(s32[2,8,2,16]{3,2,1,0:T(2,128)} %request_ref.5) | copy-start | bytes 6148
  0.7 1.1 %copy-start.2 = (s32[2,512]{1,0:T(2,128)S(1)}, s32[2,512]{1,0:T(2,128)}, u32[]{:S(2)}) copy-start(s32[2,512]{1,0:T(2,128)} %own_neg_ref.3) | copy-start | bytes 12292
  0.7 1.1 %copy-start.3 = (s32[2,512]{1,0:T(2,128)S(1)}, s32[2,512]{1,0:T(2,128)}, u32[]{:S(2)}) copy-start(s32[2,512]{1,0:T(2,128)} %far_neg_ref.3) | copy-start | bytes 12292
  0.7 1.1 %copy-start.4 = (s32[2,128]{1,0:T(2,128)S(1)}, s32[2,128]{1,0:T(2,128)}, u32[]{:S(2)}) copy-start(s32[2,128]{1,0:T(2,128)} %head_ref.5) | copy-start | bytes 3076
  0.7 1.1 %copy-start.5 = (s32[2,128]{1,0:T(2,128)S(1)}, s32[2,128]{1,0:T(2,128)}, u32[]{:S(2)}) copy-start(s32[2,128]{1,0:T(2,128)} %tail_ref.5) | copy-start | bytes 3076
  0.7 1.1 %copy-start.6 = (s32[2,128]{1,0:T(2,128)S(1)}, s32[2,128]{1,0:T(2,128)}, u32[]{:S(2)}) copy-start(s32[2,128]{1,0:T(2,128)} %rel_ref.5) | copy-start | bytes 3076
  43.0 1.4 %collective-permute-start = (bf16[128,272]{1,0:T(8,128)(2,1)S(1)}, bf16[128,272]{1,0:T(8,128)(2,1)S(1)}, u32[]{:S(2)}, u32[]{:S(2)}) collective-permute-start(bf16[128,272]{1,0:T(8,128)(2,1)S(1)} %bitcast.21), channel_id=1, source_target_pairs={{0,8},{8,0},{16,24},{24,16},{1,9},{9,1},{17,25},{25,17},{2,10},{10... | collective-permute-start | bytes 208904 | tf_op jit(solution)/shard_map/ppermute | solution.py:433
where the time goes:
time: 59.7 us; the launch traced here: 59.4 us
  blocking collectives  52.2 us (87%)
  Pallas kernels  4.49 us (8%)
  other arithmetic  1.04 us (2%)
  waiting for transfers between devices  0.86 us (1%)
  between operations  0.79 us (1%)
    all_to_all x4, blocking collectives, swap_pair(): lax.all_to_all(value, ('dom', 'shard'), split_axis=0, concat_axis=0, axis...  52.2 us
    pallas_call x7, Pallas kernels, call(): pl.pallas_call(kernel, out_shape=[jax.ShapeDtypeStruct(shape, kind) for s...  4.49 us
  transfers between devices with their start and end apart: 1, of which 1 were waited for; matrix products, arithmetic and copies ran while one was open for 0% of the time, Pallas kernels for 1%

commit v1 on v0

--- a/solution.py
+++ b/solution.py
@@ -46,21 +46,18 @@
     return jnp.sum(jnp.where(iota((n, n), 0) == iota((n, n), 1), column, 0.0), axis=0, keepdims=True)
 
 
-def reverse(index, count):
-    return (count - 1) ^ index
-
-
-def spread_order(shards):
-    return [reverse(s, shards) for s in range(shards)]
+def turn(index, count, r):
+    swap = (index >> 1 ^ index >> 2) & 1 if r and count >= 8 else 0
+    return (count - 1) ^ index ^ swap * 6
 
 
 def group_bit(r):
     return 1 - ((lax.axis_index("dom") >> r) & 1)
 
 
-def renumber(slot, shards, slots):
+def renumber(slot, shards, slots, r):
     half = slots // 2
-    return (slot // half % 2) * (shards * half) + reverse(slot // slots, shards) * half + slot % half
+    return (slot // half % 2) * (shards * half) + turn(slot // slots, shards, r) * half + slot % half
 
 
 def halves(ref, r):
@@ -102,7 +99,7 @@
     flip = group_bit(r) == 1
     rep = jnp.concatenate(
         [
-            jnp.broadcast_to(ids[reverse(place, shards)][None], (half, slots))
+            jnp.broadcast_to(ids[turn(place, shards, r)][None], (half, slots))
             for ids in (jnp.where(flip, sides[1], sides[0]), jnp.where(flip, sides[0], sides[1]))
             for place in range(shards)
         ],
@@ -198,14 +195,14 @@
     far = unfold(rec_ref[far_half], width)
     row = slice(r, r + 1)
     ids = rel_ref[row]
-    heads, tails = renumber(head_ref[row], shards, slots), renumber(tail_ref[row], shards, slots)
+    heads, tails = renumber(head_ref[row], shards, slots, r), renumber(tail_ref[row], shards, slots, r)
     head = dot(one_hot(to_column(heads), touched), own)
     tail = dot(one_hot(to_column(tails), touched), far)
     rel = dot(one_hot(to_column(ids), relations_ref.shape[0]), relations_ref[...])
     query_tail, query_head, coeff = by_blocks(query_block, head, tail, rel)
 
     def weights(query, rows, neg_ref):
-        hit = iota((touched, negatives), 0) == renumber(neg_ref[row], shards, slots)
+        hit = iota((touched, negatives), 0) == renumber(neg_ref[row], shards, slots, r)
         scale = jnp.sum(jnp.where(hit, 1.0 / negatives, 0.0), axis=1, keepdims=True)
         return jax.nn.sigmoid(dot(query, rows, LAST)) * to_row(scale)
 
@@ -244,7 +241,7 @@
     ids = jnp.concatenate([rel_ref[r : r + 1] for r in range(rel_ref.shape[0])], axis=1)
     owner = ids // per_device
     dom = owner // shards
-    chunk = (1 - (dom >> bit & 1)) * shards + reverse(owner % shards, shards)
+    chunk = (1 - (dom >> bit & 1)) * shards + turn(owner % shards, shards, bit)
     meant = (dom ^ lax.axis_index("dom") ^ mask) & ~(1 << bit) == 0
     rows_each = rows // (2 * shards)
     spot, free = ids % per_device, rows_each - per_device
@@ -295,7 +292,7 @@
 ):
     shards, slots = lax.axis_size("shard"), slots_of(out_ref)
     for side, (half, slot_ref) in enumerate(zip(halves(out_ref, bit), (head_ref, tail_ref))):
-        slot = renumber(slot_ref[bit : bit + 1], shards, slots)
+        slot = renumber(slot_ref[bit : bit + 1], shards, slots, bit)
         out_ref[half] = row_grads(slot, weights_ref[side].astype(F32), right_ref[side])
     sums_out[...] = relation_sums(rel_ref, values_ref[...], bit, per_device, 0, out_ref.shape[0])
     hot_out[...] = request_hot(request_ref, bit, hot_out.shape[0]).astype(F32).T.astype(BF16)
@@ -365,9 +362,8 @@
 
 def swap_pair(value, r):
     doms, shards = lax.axis_size("dom"), lax.axis_size("shard")
-    order = spread_order(shards)
     groups = [
-        [g * shards + s for g in (low ^ (1 << r), low) for s in sorted(range(shards), key=order.__getitem__)]
+        [g * shards + turn(place, shards, r) for g in (low ^ (1 << r), low) for place in range(shards)]
         for low in range(doms)
         if not low >> r & 1
     ]

time: 59.7 us -> 60.4 us (1.012)
    all_to_all x4, blocking collectives: 52.2 us -> 52.8 us  [swap_pair(): lax.all_to_all(value, ('dom', 'shard'), split_axis=0, concat_axis=0, axis...]
where the time goes in v1:
time: 60.4 us; the launch traced here: 60.1 us
  blocking collectives  52.8 us (87%)
  Pallas kernels  4.5 us (7%)
  other arithmetic  1.04 us (2%)
  waiting for transfers between devices  0.85 us (1%)
  between operations  0.79 us (1%)
    all_to_all x4, blocking collectives, swap_pair(): lax.all_to_all(value, ('dom', 'shard'), split_axis=0, concat_axis=0, axis...  52.8 us
    pallas_call x7, Pallas kernels, call(): pl.pallas_call(kernel, out_shape=[jax.ShapeDtypeStruct(shape, kind) for s...  4.5 us
  transfers between devices with their start and end apart: 1, of which 1 were waited for; matrix products, arithmetic and copies ran while one was open for 0% of the time, Pallas kernels for 1%

profile of v1, /device:TPU:0, one launch (start us, length us, event | category | flops | bytes accessed | tf_op | source)
XLA Modules:
  0.0 60.1 jit_solution(17241538905216201045)
XLA Ops:
  0.6 0.0 copy-start
  0.6 0.0 copy-start.1
  0.7 0.0 copy-start.2
  0.7 0.0 copy-start.3
  0.7 0.0 copy-start.4
  0.7 0.0 copy-start.5
  0.7 0.0 copy-start.6
  0.7 1.0 %pad_add_fusion.state_ref = f32[66,400]{1,0:T(8,128)S(1)} fusion(f32[1,5]{1,0:T(1,128)} %bitcast.22, f32[1,64]{1,0:T(1,128)} %bitcast.23, f32[64,400]{1,0:T(8,128)} %param.10), kind=kLoop, calls=%fused_computation | loop fusion | flops 52800 | bytes 208276 | tf_op jit(solution)/shard_map/add | solution.py:398
  1.7 0.0 copy-done
  1.8 0.0 copy-done.1
  1.8 0.0 copy-done.2
  1.8 0.0 copy-done.3
  1.8 0.0 copy-done.4
  1.8 0.0 copy-done.5
  1.8 0.0 copy-done.6
  1.8 0.4 shard_map.129
  2.2 13.8 %all_to_all.44 = bf16[16,8,800]{2,1,0:T(8,128)(2,1)S(1)} all-to-all(bf16[16,8,800]{2,1,0:T(8,128)(2,1)S(1)} %bitcast.16), channel_id=1, replica_groups={{15,14,13,12,11,10,9,8,7,6,5,4,3,2,1,0},{31,30,29,28,27,26,25,24,23,22,..., dimensions={0} | all-to-all | bytes 409600 | tf_op jit(solution)/shard_map/all_to_all | solution.py:370
  16.0 1.0 %shard_map.130 = (bf16[128,800]{1,0:T(8,128)(2,1)S(1)}, bf16[128,400]{1,0:T(8,128)(2,1)S(1)}) custom-call(bf16[128,800]{1,0:T(8,128)(2,1)S(1)} %bitcast.15, s32[2,128]{1,0:T(2,128)S(1)} %copy-done.4, s32[2,128]{1,0:T(2,128)S(1)} %copy-done.5, s32[2,128]{1,0:T(2,128)S(1)} %copy-done.6, s32[2,512]{1,0:T(2,128)S(1)} %copy-done.2, s32[2,512]{1,0:T(2,128)S(1)} %copy-done.3, ...), custom_call_target="tpu_custom_call" | custom-call | tf_op jit(solution)/shard_map/pallas_call | solution.py:355
  17.1 11.6 %all_to_all.45 = bf16[16,8,800]{2,1,0:T(8,128)(2,1)S(1)} all-to-all(bf16[16,8,800]{2,1,0:T(8,128)(2,1)S(1)} %bitcast.20), channel_id=1, replica_groups={{15,14,13,12,11,10,9,8,7,6,5,4,3,2,1,0},{31,30,29,28,27,26,25,24,23,22,..., dimensions={0} | all-to-all | bytes 409600 | tf_op jit(solution)/shard_map/all_to_all | solution.py:370
  28.6 0.6 shard_map.131
  29.2 13.2 %all_to_all.46 = bf16[16,8,800]{2,1,0:T(8,128)(2,1)S(1)} all-to-all(bf16[16,8,800]{2,1,0:T(8,128)(2,1)S(1)} %bitcast.19), channel_id=1, replica_groups={{23,22,19,18,21,20,17,16,7,6,3,2,5,4,1,0},{31,30,27,26,29,28,25,24,15,1..., dimensions={0} | all-to-all | bytes 409600 | tf_op jit(solution)/shard_map/all_to_all | solution.py:370
  42.4 1.0 %shard_map.132 = (bf16[2,128,128]{2,1,0:T(8,128)(2,1)S(1)}, bf16[2,256,400]{2,1,0:T(8,128)(2,1)S(1)}, bf16[256,400]{1,0:T(8,128)(2,1)S(1)}, bf16[1,128,272]{2,1,0:T(8,128)(2,1)S(1)}) custom-call(bf16[128,800]{1,0:T(8,128)(2,1)S(1)} %bitcast.17, s32[2,128]{1,0:T(2,128)S(1)} %copy-done.4, s32[2,128]{1,0:T(2,128)S(1)} %copy-done.5, s32[2,128]{1,0:T(2,128)S(1)} %copy-done.6, ...), custom_call_target="tpu_custom_call" | custom-call | tf_op jit(solution)/shard_map/pallas_call | solution.py:355
  43.4 0.1 collective-permute-start
  43.4 0.4 shard_map.133
  43.9 0.9 %collective-permute-done.refs_0_ = bf16[128,272]{1,0:T(8,128)(2,1)S(1)} collective-permute-done((bf16[128,272]{1,0:T(8,128)(2,1)S(1)}, bf16[128,272]{1,0:T(8,128)(2,1)S(1)}, u32[]{:S(2)}, u32[]{:S(2)}) %collective-permute-start) | collective-permute-done | bytes 69664 | tf_op jit(solution)/shard_map/ppermute | solution.py:429
  44.7 0.1 shard_map.134
  44.8 14.2 %all_to_all.47 = bf16[16,8,1152]{2,1,0:T(8,128)(2,1)S(1)} all-to-all(bf16[16,8,1152]{2,1,0:T(8,128)(2,1)S(1)} %bitcast.13), channel_id=1, replica_groups={{23,22,19,18,21,20,17,16,7,6,3,2,5,4,1,0},{31,30,27,26,29,28,25,24,15,1..., dimensions={0} | all-to-all | bytes 589824 | tf_op jit(solution)/shard_map/all_to_all | solution.py:370
  59.1 1.0 %shard_map.135 = (f32[64,400]{1,0:T(8,128)}, f32[1,64]{1,0:T(1,128)}, f32[5,400]{1,0:T(8,128)}, f32[1,5]{1,0:T(1,128)}) custom-call(bf16[64,256]{1,0:T(8,128)(2,1)S(1)} %get-tuple-element.25.hot_ref, bf16[128,1152]{1,0:T(8,128)(2,1)S(1)} %bitcast.14, f32[66,400]{1,0:T(8,128)S(1)} %get-tuple-element.29.state_ref), custom_call_target="tpu_custom_call" | custom-call | tf_op jit(solution)/shard_map/pallas_call | solution.py:355
Async XLA Ops:
  0.6 1.1 %copy-start = (bf16[160,400]{1,0:T(8,128)(2,1)S(1)}, bf16[160,400]{1,0:T(8,128)(2,1)}, u32[]{:S(2)}) copy-start(bf16[160,400]{1,0:T(8,128)(2,1)} %relations_ref.3) | copy-start | bytes 384004
  0.6 1.1 %copy-start.1 = (s32[2,8,2,16]{3,2,1,0:T(2,128)S(1)}, s32[2,8,2,16]{3,2,1,0:T(2,128)}, u32[]{:S(2)}) copy-start(s32[2,8,2,16]{3,2,1,0:T(2,128)} %request_ref.5) | copy-start | bytes 6148
  0.7 1.1 %copy-start.2 = (s32[2,512]{1,0:T(2,128)S(1)}, s32[2,512]{1,0:T(2,128)}, u32[]{:S(2)}) copy-start(s32[2,512]{1,0:T(2,128)} %own_neg_ref.3) | copy-start | bytes 12292
  0.7 1.1 %copy-start.3 = (s32[2,512]{1,0:T(2,128)S(1)}, s32[2,512]{1,0:T(2,128)}, u32[]{:S(2)}) copy-start(s32[2,512]{1,0:T(2,128)} %far_neg_ref.3) | copy-start | bytes 12292
  0.7 1.1 %copy-start.4 = (s32[2,128]{1,0:T(2,128)S(1)}, s32[2,128]{1,0:T(2,128)}, u32[]{:S(2)}) copy-start(s32[2,128]{1,0:T(2,128)} %head_ref.5) | copy-start | bytes 3076
  0.7 1.1 %copy-start.5 = (s32[2,128]{1,0:T(2,128)S(1)}, s32[2,128]{1,0:T(2,128)}, u32[]{:S(2)}) copy-start(s32[2,128]{1,0:T(2,128)} %tail_ref.5) | copy-start | bytes 3076
  0.7 1.1 %copy-start.6 = (s32[2,128]{1,0:T(2,128)S(1)}, s32[2,128]{1,0:T(2,128)}, u32[]{:S(2)}) copy-start(s32[2,128]{1,0:T(2,128)} %rel_ref.5) | copy-start | bytes 3076
  43.4 1.4 %collective-permute-start = (bf16[128,272]{1,0:T(8,128)(2,1)S(1)}, bf16[128,272]{1,0:T(8,128)(2,1)S(1)}, u32[]{:S(2)}, u32[]{:S(2)}) collective-permute-start(bf16[128,272]{1,0:T(8,128)(2,1)S(1)} %bitcast.21), channel_id=1, source_target_pairs={{0,8},{8,0},{16,24},{24,16},{1,9},{9,1},{17,25},{25,17},{2,10},{10... | collective-permute-start | bytes 208904 | tf_op jit(solution)/shard_map/ppermute | solution.py:429

commit v2 on v0

--- a/solution.py
+++ b/solution.py
@@ -205,9 +205,11 @@
     query_tail, query_head, coeff = by_blocks(query_block, head, tail, rel)
 
     def weights(query, rows, neg_ref):
-        hit = iota((touched, negatives), 0) == renumber(neg_ref[row], shards, slots)
-        scale = jnp.sum(jnp.where(hit, 1.0 / negatives, 0.0), axis=1, keepdims=True)
-        return jax.nn.sigmoid(dot(query, rows, LAST)) * to_row(scale)
+        hit = one_hot_t(renumber(neg_ref[row], shards, slots), touched)
+        counts = dot(hit, jnp.ones((negatives, touched), BF16))
+        same = iota((touched, touched), 0) == iota((touched, touched), 1)
+        scale = jnp.sum(jnp.where(same, counts, 0.0), axis=0, keepdims=True) * (1.0 / negatives)
+        return jax.nn.sigmoid(dot(query, rows, LAST)) * scale
 
     weight_tail = weights(query_tail, far, far_neg_ref)
     weight_head = weights(query_head, own, own_neg_ref)

time: 59.7 us -> 59.7 us (level)
  no operation moved by 1% of the time
where the time goes in v2:
time: 59.7 us; the launch traced here: 59.4 us
  blocking collectives  52.2 us (87%)
  Pallas kernels  4.45 us (7%)
  other arithmetic  1.04 us (2%)
  waiting for transfers between devices  0.86 us (1%)
  between operations  0.79 us (1%)
    all_to_all x4, blocking collectives, swap_pair(): lax.all_to_all(value, ('dom', 'shard'), split_axis=0, concat_axis=0, axis...  52.2 us
    pallas_call x7, Pallas kernels, call(): pl.pallas_call(kernel, out_shape=[jax.ShapeDtypeStruct(shape, kind) for s...  4.45 us
  transfers between devices with their start and end apart: 1, of which 1 were waited for; matrix products, arithmetic and copies ran while one was open for 0% of the time, Pallas kernels for 1%

profile of v2, /device:TPU:0, one launch (start us, length us, event | category | flops | bytes accessed | tf_op | source)
XLA Modules:
  0.0 59.4 jit_solution(3767040083586969141)
XLA Ops:
  0.6 0.0 copy-start
  0.6 0.0 copy-start.1
  0.7 0.0 copy-start.2
  0.7 0.0 copy-start.3
  0.7 0.0 copy-start.4
  0.7 0.0 copy-start.5
  0.7 0.0 copy-start.6
  0.7 1.0 %pad_add_fusion.state_ref = f32[66,400]{1,0:T(8,128)S(1)} fusion(f32[1,5]{1,0:T(1,128)} %bitcast.22, f32[1,64]{1,0:T(1,128)} %bitcast.23, f32[64,400]{1,0:T(8,128)} %param.10), kind=kLoop, calls=%fused_computation | loop fusion | flops 52800 | bytes 208276 | tf_op jit(solution)/shard_map/add | solution.py:404
  1.7 0.0 copy-done
  1.8 0.0 copy-done.1
  1.8 0.0 copy-done.2
  1.8 0.0 copy-done.3
  1.8 0.0 copy-done.4
  1.8 0.0 copy-done.5
  1.8 0.0 copy-done.6
  1.8 0.4 shard_map.129
  2.2 13.8 %all_to_all.44 = bf16[16,8,800]{2,1,0:T(8,128)(2,1)S(1)} all-to-all(bf16[16,8,800]{2,1,0:T(8,128)(2,1)S(1)} %bitcast.16), channel_id=1, replica_groups={{15,14,13,12,11,10,9,8,7,6,5,4,3,2,1,0},{31,30,29,28,27,26,25,24,23,22,..., dimensions={0} | all-to-all | bytes 409600 | tf_op jit(solution)/shard_map/all_to_all | solution.py:376
  16.0 1.0 %shard_map.130 = (bf16[128,800]{1,0:T(8,128)(2,1)S(1)}, bf16[128,400]{1,0:T(8,128)(2,1)S(1)}) custom-call(bf16[128,800]{1,0:T(8,128)(2,1)S(1)} %bitcast.15, s32[2,128]{1,0:T(2,128)S(1)} %copy-done.4, s32[2,128]{1,0:T(2,128)S(1)} %copy-done.5, s32[2,128]{1,0:T(2,128)S(1)} %copy-done.6, s32[2,512]{1,0:T(2,128)S(1)} %copy-done.2, s32[2,512]{1,0:T(2,128)S(1)} %copy-done.3, ...), custom_call_target="tpu_custom_call" | custom-call | tf_op jit(solution)/shard_map/pallas_call | solution.py:360
  17.0 11.6 %all_to_all.45 = bf16[16,8,800]{2,1,0:T(8,128)(2,1)S(1)} all-to-all(bf16[16,8,800]{2,1,0:T(8,128)(2,1)S(1)} %bitcast.20), channel_id=1, replica_groups={{15,14,13,12,11,10,9,8,7,6,5,4,3,2,1,0},{31,30,29,28,27,26,25,24,23,22,..., dimensions={0} | all-to-all | bytes 409600 | tf_op jit(solution)/shard_map/all_to_all | solution.py:376
  28.6 0.6 %shard_map.131 = (f32[66,400]{1,0:T(8,128)S(1)}, bf16[128,800]{1,0:T(8,128)(2,1)S(1)}) custom-call(s32[2,8,2,16]{3,2,1,0:T(2,128)S(1)} %copy-done.1, bf16[128,800]{1,0:T(8,128)(2,1)S(1)} %bitcast.18, f32[66,400]{1,0:T(8,128)S(1)} %pad_add_fusion.state_ref), custom_call_target="tpu_custom_call" | custom-call | tf_op jit(solution)/shard_map/pallas_call | solution.py:360
  29.2 12.8 %all_to_all.46 = bf16[16,8,800]{2,1,0:T(8,128)(2,1)S(1)} all-to-all(bf16[16,8,800]{2,1,0:T(8,128)(2,1)S(1)} %bitcast.19), channel_id=1, replica_groups={{23,22,21,20,19,18,17,16,7,6,5,4,3,2,1,0},{31,30,29,28,27,26,25,24,15,1..., dimensions={0} | all-to-all | bytes 409600 | tf_op jit(solution)/shard_map/all_to_all | solution.py:376
  42.0 0.9 %shard_map.132 = (bf16[2,128,128]{2,1,0:T(8,128)(2,1)S(1)}, bf16[2,256,400]{2,1,0:T(8,128)(2,1)S(1)}, bf16[256,400]{1,0:T(8,128)(2,1)S(1)}, bf16[1,128,272]{2,1,0:T(8,128)(2,1)S(1)}) custom-call(bf16[128,800]{1,0:T(8,128)(2,1)S(1)} %bitcast.17, s32[2,128]{1,0:T(2,128)S(1)} %copy-done.4, s32[2,128]{1,0:T(2,128)S(1)} %copy-done.5, s32[2,128]{1,0:T(2,128)S(1)} %copy-done.6, ...), custom_call_target="tpu_custom_call" | custom-call | tf_op jit(solution)/shard_map/pallas_call | solution.py:360
  42.9 0.1 collective-permute-start
  43.0 0.4 shard_map.133
  43.5 0.9 %collective-permute-done.refs_0_ = bf16[128,272]{1,0:T(8,128)(2,1)S(1)} collective-permute-done((bf16[128,272]{1,0:T(8,128)(2,1)S(1)}, bf16[128,272]{1,0:T(8,128)(2,1)S(1)}, u32[]{:S(2)}, u32[]{:S(2)}) %collective-permute-start) | collective-permute-done | bytes 69664 | tf_op jit(solution)/shard_map/ppermute | solution.py:435
  44.3 0.1 shard_map.134
  44.4 14.0 %all_to_all.47 = bf16[16,8,1152]{2,1,0:T(8,128)(2,1)S(1)} all-to-all(bf16[16,8,1152]{2,1,0:T(8,128)(2,1)S(1)} %bitcast.13), channel_id=1, replica_groups={{23,22,21,20,19,18,17,16,7,6,5,4,3,2,1,0},{31,30,29,28,27,26,25,24,15,1..., dimensions={0} | all-to-all | bytes 589824 | tf_op jit(solution)/shard_map/all_to_all | solution.py:376
  58.4 1.0 %shard_map.135 = (f32[64,400]{1,0:T(8,128)}, f32[1,64]{1,0:T(1,128)}, f32[5,400]{1,0:T(8,128)}, f32[1,5]{1,0:T(1,128)}) custom-call(bf16[64,256]{1,0:T(8,128)(2,1)S(1)} %get-tuple-element.25.hot_ref, bf16[128,1152]{1,0:T(8,128)(2,1)S(1)} %bitcast.14, f32[66,400]{1,0:T(8,128)S(1)} %get-tuple-element.29.state_ref), custom_call_target="tpu_custom_call" | custom-call | tf_op jit(solution)/shard_map/pallas_call | solution.py:360
Async XLA Ops:
  0.6 1.1 %copy-start = (bf16[160,400]{1,0:T(8,128)(2,1)S(1)}, bf16[160,400]{1,0:T(8,128)(2,1)}, u32[]{:S(2)}) copy-start(bf16[160,400]{1,0:T(8,128)(2,1)} %relations_ref.3) | copy-start | bytes 384004
  0.6 1.1 %copy-start.1 = (s32[2,8,2,16]{3,2,1,0:T(2,128)S(1)}, s32[2,8,2,16]{3,2,1,0:T(2,128)}, u32[]{:S(2)}) copy-start(s32[2,8,2,16]{3,2,1,0:T(2,128)} %request_ref.5) | copy-start | bytes 6148
  0.7 1.1 %copy-start.2 = (s32[2,512]{1,0:T(2,128)S(1)}, s32[2,512]{1,0:T(2,128)}, u32[]{:S(2)}) copy-start(s32[2,512]{1,0:T(2,128)} %own_neg_ref.3) | copy-start | bytes 12292
  0.7 1.1 %copy-start.3 = (s32[2,512]{1,0:T(2,128)S(1)}, s32[2,512]{1,0:T(2,128)}, u32[]{:S(2)}) copy-start(s32[2,512]{1,0:T(2,128)} %far_neg_ref.3) | copy-start | bytes 12292
  0.7 1.1 %copy-start.4 = (s32[2,128]{1,0:T(2,128)S(1)}, s32[2,128]{1,0:T(2,128)}, u32[]{:S(2)}) copy-start(s32[2,128]{1,0:T(2,128)} %head_ref.5) | copy-start | bytes 3076
  0.7 1.1 %copy-start.5 = (s32[2,128]{1,0:T(2,128)S(1)}, s32[2,128]{1,0:T(2,128)}, u32[]{:S(2)}) copy-start(s32[2,128]{1,0:T(2,128)} %tail_ref.5) | copy-start | bytes 3076
  0.7 1.1 %copy-start.6 = (s32[2,128]{1,0:T(2,128)S(1)}, s32[2,128]{1,0:T(2,128)}, u32[]{:S(2)}) copy-start(s32[2,128]{1,0:T(2,128)} %rel_ref.5) | copy-start | bytes 3076
  42.9 1.4 %collective-permute-start = (bf16[128,272]{1,0:T(8,128)(2,1)S(1)}, bf16[128,272]{1,0:T(8,128)(2,1)S(1)}, u32[]{:S(2)}, u32[]{:S(2)}) collective-permute-start(bf16[128,272]{1,0:T(8,128)(2,1)S(1)} %bitcast.21), channel_id=1, source_target_pairs={{0,8},{8,0},{16,24},{24,16},{1,9},{9,1},{17,25},{25,17},{2,10},{10... | collective-permute-start | bytes 208904 | tf_op jit(solution)/shard_map/ppermute | solution.py:435

commit v3 on v2

--- a/solution.py
+++ b/solution.py
@@ -336,9 +336,7 @@
     copies = [pltpu.make_async_copy(source, target, sems.at[i]) for i, (source, target) in enumerate(pairs)]
     table, accum = row_update(hot_ref[...], back_ref, state_ref, NATURAL)
     table_ref[...] = table
-    copies[0].start()
     row_accum_ref[...] = accum
-    copies[1].start()
     per_device, width = step_ref.shape
     rows = slots_of(back_ref) // 2
     tiles, rest = 2 * whole(width), width - whole(width)
@@ -349,9 +347,9 @@
     grad = unpack_sums(total, per_device)
     accum = to_column(state_ref[table.shape[0] + 1 :, :per_device]) + jnp.mean(grad * grad, axis=1, keepdims=True)
     step_ref[...] = grad * (-LEARN_RATE * lax.rsqrt(accum))
-    copies[2].start()
     new_accum_ref[...] = to_row(accum)
-    copies[3].start()
+    for copy in copies:
+        copy.start()
     for copy in copies:
         copy.wait()
 

time: 59.7 us -> 59.7 us (level)
  no operation moved by 1% of the time
where the time goes in v3:
time: 59.7 us; the launch traced here: 59.4 us
  blocking collectives  52.2 us (87%)
  Pallas kernels  4.45 us (7%)
  other arithmetic  1.04 us (2%)
  waiting for transfers between devices  0.86 us (1%)
  between operations  0.79 us (1%)
    all_to_all x4, blocking collectives, swap_pair(): lax.all_to_all(value, ('dom', 'shard'), split_axis=0, concat_axis=0, axis...  52.2 us
    pallas_call x7, Pallas kernels, call(): pl.pallas_call(kernel, out_shape=[jax.ShapeDtypeStruct(shape, kind) for s...  4.45 us
  transfers between devices with their start and end apart: 1, of which 1 were waited for; matrix products, arithmetic and copies ran while one was open for 0% of the time, Pallas kernels for 1%

profile of v3, /device:TPU:0, one launch (start us, length us, event | category | flops | bytes accessed | tf_op | source)
XLA Modules:
  0.0 59.4 jit_solution(3767040083586969141)
XLA Ops:
  0.6 0.0 copy-start
  0.6 0.0 copy-start.1
  0.7 0.0 copy-start.2
  0.7 0.0 copy-start.3
  0.7 0.0 copy-start.4
  0.7 0.0 copy-start.5
  0.7 0.0 copy-start.6
  0.7 1.0 %pad_add_fusion.state_ref = f32[66,400]{1,0:T(8,128)S(1)} fusion(f32[1,5]{1,0:T(1,128)} %bitcast.22, f32[1,64]{1,0:T(1,128)} %bitcast.23, f32[64,400]{1,0:T(8,128)} %param.10), kind=kLoop, calls=%fused_computation | loop fusion | flops 52800 | bytes 208276 | tf_op jit(solution)/shard_map/add | solution.py:402
  1.7 0.0 copy-done
  1.8 0.0 copy-done.1
  1.8 0.0 copy-done.2
  1.8 0.0 copy-done.3
  1.8 0.0 copy-done.4
  1.8 0.0 copy-done.5
  1.8 0.0 copy-done.6
  1.8 0.4 shard_map.129
  2.2 13.8 %all_to_all.44 = bf16[16,8,800]{2,1,0:T(8,128)(2,1)S(1)} all-to-all(bf16[16,8,800]{2,1,0:T(8,128)(2,1)S(1)} %bitcast.16), channel_id=1, replica_groups={{15,14,13,12,11,10,9,8,7,6,5,4,3,2,1,0},{31,30,29,28,27,26,25,24,23,22,..., dimensions={0} | all-to-all | bytes 409600 | tf_op jit(solution)/shard_map/all_to_all | solution.py:374
  16.0 1.0 %shard_map.130 = (bf16[128,800]{1,0:T(8,128)(2,1)S(1)}, bf16[128,400]{1,0:T(8,128)(2,1)S(1)}) custom-call(bf16[128,800]{1,0:T(8,128)(2,1)S(1)} %bitcast.15, s32[2,128]{1,0:T(2,128)S(1)} %copy-done.4, s32[2,128]{1,0:T(2,128)S(1)} %copy-done.5, s32[2,128]{1,0:T(2,128)S(1)} %copy-done.6, s32[2,512]{1,0:T(2,128)S(1)} %copy-done.2, s32[2,512]{1,0:T(2,128)S(1)} %copy-done.3, ...), custom_call_target="tpu_custom_call" | custom-call | tf_op jit(solution)/shard_map/pallas_call | solution.py:358
  17.0 11.6 %all_to_all.45 = bf16[16,8,800]{2,1,0:T(8,128)(2,1)S(1)} all-to-all(bf16[16,8,800]{2,1,0:T(8,128)(2,1)S(1)} %bitcast.20), channel_id=1, replica_groups={{15,14,13,12,11,10,9,8,7,6,5,4,3,2,1,0},{31,30,29,28,27,26,25,24,23,22,..., dimensions={0} | all-to-all | bytes 409600 | tf_op jit(solution)/shard_map/all_to_all | solution.py:374
  28.6 0.6 %shard_map.131 = (f32[66,400]{1,0:T(8,128)S(1)}, bf16[128,800]{1,0:T(8,128)(2,1)S(1)}) custom-call(s32[2,8,2,16]{3,2,1,0:T(2,128)S(1)} %copy-done.1, bf16[128,800]{1,0:T(8,128)(2,1)S(1)} %bitcast.18, f32[66,400]{1,0:T(8,128)S(1)} %pad_add_fusion.state_ref), custom_call_target="tpu_custom_call" | custom-call | tf_op jit(solution)/shard_map/pallas_call | solution.py:358
  29.2 12.8 %all_to_all.46 = bf16[16,8,800]{2,1,0:T(8,128)(2,1)S(1)} all-to-all(bf16[16,8,800]{2,1,0:T(8,128)(2,1)S(1)} %bitcast.19), channel_id=1, replica_groups={{23,22,21,20,19,18,17,16,7,6,5,4,3,2,1,0},{31,30,29,28,27,26,25,24,15,1..., dimensions={0} | all-to-all | bytes 409600 | tf_op jit(solution)/shard_map/all_to_all | solution.py:374
  42.0 0.9 %shard_map.132 = (bf16[2,128,128]{2,1,0:T(8,128)(2,1)S(1)}, bf16[2,256,400]{2,1,0:T(8,128)(2,1)S(1)}, bf16[256,400]{1,0:T(8,128)(2,1)S(1)}, bf16[1,128,272]{2,1,0:T(8,128)(2,1)S(1)}) custom-call(bf16[128,800]{1,0:T(8,128)(2,1)S(1)} %bitcast.17, s32[2,128]{1,0:T(2,128)S(1)} %copy-done.4, s32[2,128]{1,0:T(2,128)S(1)} %copy-done.5, s32[2,128]{1,0:T(2,128)S(1)} %copy-done.6, ...), custom_call_target="tpu_custom_call" | custom-call | tf_op jit(solution)/shard_map/pallas_call | solution.py:358
  42.9 0.1 collective-permute-start
  43.0 0.4 shard_map.133
  43.5 0.9 %collective-permute-done.refs_0_ = bf16[128,272]{1,0:T(8,128)(2,1)S(1)} collective-permute-done((bf16[128,272]{1,0:T(8,128)(2,1)S(1)}, bf16[128,272]{1,0:T(8,128)(2,1)S(1)}, u32[]{:S(2)}, u32[]{:S(2)}) %collective-permute-start) | collective-permute-done | bytes 69664 | tf_op jit(solution)/shard_map/ppermute | solution.py:433
  44.3 0.1 shard_map.134
  44.4 14.0 %all_to_all.47 = bf16[16,8,1152]{2,1,0:T(8,128)(2,1)S(1)} all-to-all(bf16[16,8,1152]{2,1,0:T(8,128)(2,1)S(1)} %bitcast.13), channel_id=1, replica_groups={{23,22,21,20,19,18,17,16,7,6,5,4,3,2,1,0},{31,30,29,28,27,26,25,24,15,1..., dimensions={0} | all-to-all | bytes 589824 | tf_op jit(solution)/shard_map/all_to_all | solution.py:374
  58.4 1.0 %shard_map.135 = (f32[64,400]{1,0:T(8,128)}, f32[1,64]{1,0:T(1,128)}, f32[5,400]{1,0:T(8,128)}, f32[1,5]{1,0:T(1,128)}) custom-call(bf16[64,256]{1,0:T(8,128)(2,1)S(1)} %get-tuple-element.25.hot_ref, bf16[128,1152]{1,0:T(8,128)(2,1)S(1)} %bitcast.14, f32[66,400]{1,0:T(8,128)S(1)} %get-tuple-element.29.state_ref), custom_call_target="tpu_custom_call" | custom-call | tf_op jit(solution)/shard_map/pallas_call | solution.py:358
Async XLA Ops:
  0.6 1.1 %copy-start = (bf16[160,400]{1,0:T(8,128)(2,1)S(1)}, bf16[160,400]{1,0:T(8,128)(2,1)}, u32[]{:S(2)}) copy-start(bf16[160,400]{1,0:T(8,128)(2,1)} %relations_ref.3) | copy-start | bytes 384004
  0.6 1.1 %copy-start.1 = (s32[2,8,2,16]{3,2,1,0:T(2,128)S(1)}, s32[2,8,2,16]{3,2,1,0:T(2,128)}, u32[]{:S(2)}) copy-start(s32[2,8,2,16]{3,2,1,0:T(2,128)} %request_ref.5) | copy-start | bytes 6148
  0.7 1.1 %copy-start.2 = (s32[2,512]{1,0:T(2,128)S(1)}, s32[2,512]{1,0:T(2,128)}, u32[]{:S(2)}) copy-start(s32[2,512]{1,0:T(2,128)} %own_neg_ref.3) | copy-start | bytes 12292
  0.7 1.1 %copy-start.3 = (s32[2,512]{1,0:T(2,128)S(1)}, s32[2,512]{1,0:T(2,128)}, u32[]{:S(2)}) copy-start(s32[2,512]{1,0:T(2,128)} %far_neg_ref.3) | copy-start | bytes 12292
  0.7 1.1 %copy-start.4 = (s32[2,128]{1,0:T(2,128)S(1)}, s32[2,128]{1,0:T(2,128)}, u32[]{:S(2)}) copy-start(s32[2,128]{1,0:T(2,128)} %head_ref.5) | copy-start | bytes 3076
  0.7 1.1 %copy-start.5 = (s32[2,128]{1,0:T(2,128)S(1)}, s32[2,128]{1,0:T(2,128)}, u32[]{:S(2)}) copy-start(s32[2,128]{1,0:T(2,128)} %tail_ref.5) | copy-start | bytes 3076
  0.7 1.1 %copy-start.6 = (s32[2,128]{1,0:T(2,128)S(1)}, s32[2,128]{1,0:T(2,128)}, u32[]{:S(2)}) copy-start(s32[2,128]{1,0:T(2,128)} %rel_ref.5) | copy-start | bytes 3076
  42.9 1.4 %collective-permute-start = (bf16[128,272]{1,0:T(8,128)(2,1)S(1)}, bf16[128,272]{1,0:T(8,128)(2,1)S(1)}, u32[]{:S(2)}, u32[]{:S(2)}) collective-permute-start(bf16[128,272]{1,0:T(8,128)(2,1)S(1)} %bitcast.21), channel_id=1, source_target_pairs={{0,8},{8,0},{16,24},{24,16},{1,9},{9,1},{17,25},{25,17},{2,10},{10... | collective-permute-start | bytes 208904 | tf_op jit(solution)/shard_map/ppermute | solution.py:433

commit v4 on v2

--- a/solution.py
+++ b/solution.py
@@ -199,9 +199,9 @@
     row = slice(r, r + 1)
     ids = rel_ref[row]
     heads, tails = renumber(head_ref[row], shards, slots), renumber(tail_ref[row], shards, slots)
-    head = dot(one_hot(to_column(heads), touched), own)
-    tail = dot(one_hot(to_column(tails), touched), far)
-    rel = dot(one_hot(to_column(ids), relations_ref.shape[0]), relations_ref[...])
+    head = dot(one_hot_t(heads, touched), own, FIRST)
+    tail = dot(one_hot_t(tails, touched), far, FIRST)
+    rel = dot(one_hot_t(ids, relations_ref.shape[0]), relations_ref[...], FIRST)
     query_tail, query_head, coeff = by_blocks(query_block, head, tail, rel)
 
     def weights(query, rows, neg_ref):

time: 59.7 us -> 59.6 us (level)
  no operation moved by 1% of the time
where the time goes in v4:
time: 59.6 us; the launch traced here: 59.3 us
  blocking collectives  52.2 us (88%)
  Pallas kernels  4.36 us (7%)
  other arithmetic  1.04 us (2%)
  waiting for transfers between devices  0.86 us (1%)
  between operations  0.79 us (1%)
    all_to_all x4, blocking collectives, swap_pair(): lax.all_to_all(value, ('dom', 'shard'), split_axis=0, concat_axis=0, axis...  52.2 us
    pallas_call x7, Pallas kernels, call(): pl.pallas_call(kernel, out_shape=[jax.ShapeDtypeStruct(shape, kind) for s...  4.36 us
  transfers between devices with their start and end apart: 1, of which 1 were waited for; matrix products, arithmetic and copies ran while one was open for 0% of the time, Pallas kernels for 1%

profile of v4, /device:TPU:0, one launch (start us, length us, event | category | flops | bytes accessed | tf_op | source)
XLA Modules:
  0.0 59.3 jit_solution(661915054257284424)
XLA Ops:
  0.6 0.0 copy-start
  0.6 0.0 copy-start.1
  0.7 0.0 copy-start.2
  0.7 0.0 copy-start.3
  0.7 0.0 copy-start.4
  0.7 0.0 copy-start.5
  0.7 0.0 copy-start.6
  0.7 1.0 %pad_add_fusion.state_ref = f32[66,400]{1,0:T(8,128)S(1)} fusion(f32[1,5]{1,0:T(1,128)} %bitcast.22, f32[1,64]{1,0:T(1,128)} %bitcast.23, f32[64,400]{1,0:T(8,128)} %param.10), kind=kLoop, calls=%fused_computation | loop fusion | flops 52800 | bytes 208276 | tf_op jit(solution)/shard_map/add | solution.py:404
  1.7 0.0 copy-done
  1.8 0.0 copy-done.1
  1.8 0.0 copy-done.2
  1.8 0.0 copy-done.3
  1.8 0.0 copy-done.4
  1.8 0.0 copy-done.5
  1.8 0.0 copy-done.6
  1.8 0.4 shard_map.129
  2.2 13.8 %all_to_all.44 = bf16[16,8,800]{2,1,0:T(8,128)(2,1)S(1)} all-to-all(bf16[16,8,800]{2,1,0:T(8,128)(2,1)S(1)} %bitcast.16), channel_id=1, replica_groups={{15,14,13,12,11,10,9,8,7,6,5,4,3,2,1,0},{31,30,29,28,27,26,25,24,23,22,..., dimensions={0} | all-to-all | bytes 409600 | tf_op jit(solution)/shard_map/all_to_all | solution.py:376
  16.0 0.9 %shard_map.130 = (bf16[128,800]{1,0:T(8,128)(2,1)S(1)}, bf16[128,400]{1,0:T(8,128)(2,1)S(1)}) custom-call(bf16[128,800]{1,0:T(8,128)(2,1)S(1)} %bitcast.15, s32[2,128]{1,0:T(2,128)S(1)} %copy-done.4, s32[2,128]{1,0:T(2,128)S(1)} %copy-done.5, s32[2,128]{1,0:T(2,128)S(1)} %copy-done.6, s32[2,512]{1,0:T(2,128)S(1)} %copy-done.2, s32[2,512]{1,0:T(2,128)S(1)} %copy-done.3, ...), custom_call_target="tpu_custom_call" | custom-call | tf_op jit(solution)/shard_map/pallas_call | solution.py:360
  17.0 11.6 %all_to_all.45 = bf16[16,8,800]{2,1,0:T(8,128)(2,1)S(1)} all-to-all(bf16[16,8,800]{2,1,0:T(8,128)(2,1)S(1)} %bitcast.20), channel_id=1, replica_groups={{15,14,13,12,11,10,9,8,7,6,5,4,3,2,1,0},{31,30,29,28,27,26,25,24,23,22,..., dimensions={0} | all-to-all | bytes 409600 | tf_op jit(solution)/shard_map/all_to_all | solution.py:376
  28.5 0.6 %shard_map.131 = (f32[66,400]{1,0:T(8,128)S(1)}, bf16[128,800]{1,0:T(8,128)(2,1)S(1)}) custom-call(s32[2,8,2,16]{3,2,1,0:T(2,128)S(1)} %copy-done.1, bf16[128,800]{1,0:T(8,128)(2,1)S(1)} %bitcast.18, f32[66,400]{1,0:T(8,128)S(1)} %pad_add_fusion.state_ref), custom_call_target="tpu_custom_call" | custom-call | tf_op jit(solution)/shard_map/pallas_call | solution.py:360
  29.1 12.8 %all_to_all.46 = bf16[16,8,800]{2,1,0:T(8,128)(2,1)S(1)} all-to-all(bf16[16,8,800]{2,1,0:T(8,128)(2,1)S(1)} %bitcast.19), channel_id=1, replica_groups={{23,22,21,20,19,18,17,16,7,6,5,4,3,2,1,0},{31,30,29,28,27,26,25,24,15,1..., dimensions={0} | all-to-all | bytes 409600 | tf_op jit(solution)/shard_map/all_to_all | solution.py:376
  41.9 0.9 %shard_map.132 = (bf16[2,128,128]{2,1,0:T(8,128)(2,1)S(1)}, bf16[2,256,400]{2,1,0:T(8,128)(2,1)S(1)}, bf16[256,400]{1,0:T(8,128)(2,1)S(1)}, bf16[1,128,272]{2,1,0:T(8,128)(2,1)S(1)}) custom-call(bf16[128,800]{1,0:T(8,128)(2,1)S(1)} %bitcast.17, s32[2,128]{1,0:T(2,128)S(1)} %copy-done.4, s32[2,128]{1,0:T(2,128)S(1)} %copy-done.5, s32[2,128]{1,0:T(2,128)S(1)} %copy-done.6, ...), custom_call_target="tpu_custom_call" | custom-call | tf_op jit(solution)/shard_map/pallas_call | solution.py:360
  42.9 0.1 collective-permute-start
  42.9 0.4 shard_map.133
  43.4 0.9 %collective-permute-done.refs_0_ = bf16[128,272]{1,0:T(8,128)(2,1)S(1)} collective-permute-done((bf16[128,272]{1,0:T(8,128)(2,1)S(1)}, bf16[128,272]{1,0:T(8,128)(2,1)S(1)}, u32[]{:S(2)}, u32[]{:S(2)}) %collective-permute-start) | collective-permute-done | bytes 69664 | tf_op jit(solution)/shard_map/ppermute | solution.py:435
  44.2 0.1 shard_map.134
  44.3 14.0 %all_to_all.47 = bf16[16,8,1152]{2,1,0:T(8,128)(2,1)S(1)} all-to-all(bf16[16,8,1152]{2,1,0:T(8,128)(2,1)S(1)} %bitcast.13), channel_id=1, replica_groups={{23,22,21,20,19,18,17,16,7,6,5,4,3,2,1,0},{31,30,29,28,27,26,25,24,15,1..., dimensions={0} | all-to-all | bytes 589824 | tf_op jit(solution)/shard_map/all_to_all | solution.py:376
  58.3 1.0 %shard_map.135 = (f32[64,400]{1,0:T(8,128)}, f32[1,64]{1,0:T(1,128)}, f32[5,400]{1,0:T(8,128)}, f32[1,5]{1,0:T(1,128)}) custom-call(bf16[64,256]{1,0:T(8,128)(2,1)S(1)} %get-tuple-element.25.hot_ref, bf16[128,1152]{1,0:T(8,128)(2,1)S(1)} %bitcast.14, f32[66,400]{1,0:T(8,128)S(1)} %get-tuple-element.29.state_ref), custom_call_target="tpu_custom_call" | custom-call | tf_op jit(solution)/shard_map/pallas_call | solution.py:360
Async XLA Ops:
  0.6 1.1 %copy-start = (bf16[160,400]{1,0:T(8,128)(2,1)S(1)}, bf16[160,400]{1,0:T(8,128)(2,1)}, u32[]{:S(2)}) copy-start(bf16[160,400]{1,0:T(8,128)(2,1)} %relations_ref.3) | copy-start | bytes 384004
  0.6 1.1 %copy-start.1 = (s32[2,8,2,16]{3,2,1,0:T(2,128)S(1)}, s32[2,8,2,16]{3,2,1,0:T(2,128)}, u32[]{:S(2)}) copy-start(s32[2,8,2,16]{3,2,1,0:T(2,128)} %request_ref.5) | copy-start | bytes 6148
  0.7 1.1 %copy-start.2 = (s32[2,512]{1,0:T(2,128)S(1)}, s32[2,512]{1,0:T(2,128)}, u32[]{:S(2)}) copy-start(s32[2,512]{1,0:T(2,128)} %own_neg_ref.3) | copy-start | bytes 12292
  0.7 1.1 %copy-start.3 = (s32[2,512]{1,0:T(2,128)S(1)}, s32[2,512]{1,0:T(2,128)}, u32[]{:S(2)}) copy-start(s32[2,512]{1,0:T(2,128)} %far_neg_ref.3) | copy-start | bytes 12292
  0.7 1.1 %copy-start.4 = (s32[2,128]{1,0:T(2,128)S(1)}, s32[2,128]{1,0:T(2,128)}, u32[]{:S(2)}) copy-start(s32[2,128]{1,0:T(2,128)} %head_ref.5) | copy-start | bytes 3076
  0.7 1.1 %copy-start.5 = (s32[2,128]{1,0:T(2,128)S(1)}, s32[2,128]{1,0:T(2,128)}, u32[]{:S(2)}) copy-start(s32[2,128]{1,0:T(2,128)} %tail_ref.5) | copy-start | bytes 3076
  0.7 1.1 %copy-start.6 = (s32[2,128]{1,0:T(2,128)S(1)}, s32[2,128]{1,0:T(2,128)}, u32[]{:S(2)}) copy-start(s32[2,128]{1,0:T(2,128)} %rel_ref.5) | copy-start | bytes 3076
  42.9 1.4 %collective-permute-start = (bf16[128,272]{1,0:T(8,128)(2,1)S(1)}, bf16[128,272]{1,0:T(8,128)(2,1)S(1)}, u32[]{:S(2)}, u32[]{:S(2)}) collective-permute-start(bf16[128,272]{1,0:T(8,128)(2,1)S(1)} %bitcast.21), channel_id=1, source_target_pairs={{0,8},{8,0},{16,24},{24,16},{1,9},{9,1},{17,25},{25,17},{2,10},{10... | collective-permute-start | bytes 208904 | tf_op jit(solution)/shard_map/ppermute | solution.py:435
